TPU v7x, 32 devices: a whole 2x2x4 slice. The times are simulated.
32 devices in a mesh: head: 2 (over x), tm: 4 (over y, core), space: 4 (over z).
Axes of the slice: x: 2, y: 2, z: 4, core: 2. Of those that a mesh axis runs over, the one named last changes fastest.
Arguments:
- query_tiles: bfloat16 [4, 4, 4, 1, 384, 128], P('head', 'tm', 'space'), may hold values from -6 to 6
- key_tiles: bfloat16 [4, 4, 4, 1, 384, 128], P('head', 'tm', 'space'), may hold values from -6 to 6
- value_tiles: bfloat16 [4, 4, 4, 1, 384, 128], P('head', 'tm', 'space'), may hold values from -6 to 6
- out_tiles: bfloat16 [4, 4, 4, 1, 384, 128], P('head', 'tm', 'space'), may hold values from -6 to 6
- grad_tiles: bfloat16 [4, 4, 4, 1, 384, 128], P('head', 'tm', 'space'), may hold values from -6 to 6
- log_sum_exp: float32 [4, 4, 4, 1, 384], P('head', 'tm', 'space'), may hold values from 4 to 6
Outputs:
- grad_query: bfloat16 [4, 4, 4, 1, 384, 128], P('head', 'tm', 'space')
- grad_key: bfloat16 [4, 4, 4, 1, 384, 128], P('head', 'tm', 'space')
- grad_value: bfloat16 [4, 4, 4, 1, 384, 128], P('head', 'tm', 'space')
All inputs are finite; a program needn't handle non-finite values.
Results may differ from a plain program's by a relative error of at most 0.0051.
Values may be sent and summed in bfloat16 or wider, within the bound.
A program may use at most 64 MiB of HBM per device.

v0:
```python
import jax
import jax.numpy as jnp
from jax import lax
from jax.sharding import PartitionSpec as P


def extended(block, sides, width):
    for axis, dim in sides:
        count = lax.axis_size(axis)
        forward = [(i, i + 1) for i in range(count - 1)]
        backward = [(target, source) for source, target in forward]
        low = lax.ppermute(
            lax.slice_in_dim(block, block.shape[dim] - width, None, axis=dim), axis, forward
        )
        high = lax.ppermute(lax.slice_in_dim(block, 0, width, axis=dim), axis, backward)
        block = jnp.concatenate([low, block, high], axis=dim)
    return block


def shifted(value, axis, by):
    count = lax.axis_size(axis)
    pairs = [(i, i + by) for i in range(count) if 0 <= i + by < count]
    return lax.ppermute(value, axis, pairs)


def body(query_tiles, key_tiles, value_tiles, out_tiles, grad_tiles, log_sum_exp):
    head_count, _, _, column_tiles, tile_size, head_dim = query_tiles.shape
    score_scale = head_dim ** (-0.5)
    row_delta = jnp.sum(grad_tiles.astype(jnp.float32) * out_tiles.astype(jnp.float32), axis=-1)
    frame_pos = lax.axis_index("tm")
    row_pos = lax.axis_index("space")
    frame_count = lax.axis_size("tm")
    row_count = lax.axis_size("space")
    keys_ext, values_ext = (
        extended(key_tiles, (("tm", 1), ("space", 2)), 1),
        extended(value_tiles, (("tm", 1), ("space", 2)), 1),
    )
    local_query = query_tiles[:, 0, 0]
    local_grad = grad_tiles[:, 0, 0]
    local_lse = log_sum_exp[:, 0, 0]
    local_delta = row_delta[:, 0, 0]
    grad_q = jnp.zeros((head_count, column_tiles, tile_size, head_dim), jnp.float32)
    grad_k = jnp.zeros((head_count, column_tiles, tile_size, head_dim), jnp.float32)
    grad_v = jnp.zeros((head_count, column_tiles, tile_size, head_dim), jnp.float32)
    planes = [
        [
            jnp.zeros((2, head_count, column_tiles, tile_size, head_dim), jnp.float32)
            for step_r in range(3)
        ]
        for step_t in range(3)
    ]
    for step_t in range(3):
        for step_r in range(3):
            frame_near = frame_pos + step_t - 1
            row_near = row_pos + step_r - 1
            inside = (
                (frame_near >= 0)
                & (frame_near < frame_count)
                & (row_near >= 0)
                & (row_near < row_count)
            )
            weight = inside.astype(jnp.float32)
            for step_c in range(3):
                offset = step_c - 1
                begin_col = max(0, -offset)
                end_col = column_tiles - max(0, offset)
                if end_col <= begin_col:
                    continue
                near_begin = begin_col + offset
                near_end = end_col + offset
                key_part = keys_ext[:, step_t, step_r, near_begin:near_end]
                value_part = values_ext[:, step_t, step_r, near_begin:near_end]
                scores = (
                    jnp.einsum(
                        "hcqd,hckd->hcqk", local_query, key_part, preferred_element_type=jnp.float32
                    )
                    * score_scale
                )
                attention = jnp.exp(scores - local_lse[..., None]) * weight
                dprob = jnp.einsum(
                    "hcqd,hckd->hcqk", local_grad, value_part, preferred_element_type=jnp.float32
                )
                dscore = attention * (dprob - local_delta[..., None])
                attention_round = attention.astype(jnp.bfloat16)
                dscore_round = dscore.astype(jnp.bfloat16)
                grad_q = grad_q.at[:, begin_col:end_col].add(
                    jnp.einsum(
                        "hcqk,hckd->hcqd",
                        dscore_round,
                        key_part,
                        preferred_element_type=jnp.float32,
                    )
                    * score_scale
                )
                term_key = (
                    jnp.einsum(
                        "hcqk,hcqd->hckd",
                        dscore_round,
                        local_query,
                        preferred_element_type=jnp.float32,
                    )
                    * score_scale
                )
                term_value = jnp.einsum(
                    "hcqk,hcqd->hckd",
                    attention_round,
                    local_grad,
                    preferred_element_type=jnp.float32,
                )
                planes[step_t][step_r] = (
                    planes[step_t][step_r]
                    .at[:, :, near_begin:near_end]
                    .add(jnp.stack([term_key, term_value]))
                )
    frame_planes = [jnp.stack(planes[step_t], axis=2) for step_t in range(3)]
    center = frame_planes[1]
    for by_step, plane_index in ((-1, 0), (1, 2)):
        center = center + shifted(frame_planes[plane_index], "tm", by_step)
    summed = center[:, :, 1]
    for by_step, plane_index in ((-1, 0), (1, 2)):
        summed = summed + shifted(center[:, :, plane_index], "space", by_step)
    grad_k = summed[0]
    grad_v = summed[1]
    return (
        grad_q[:, None, None].astype(jnp.bfloat16),
        grad_k[:, None, None].astype(jnp.bfloat16),
        grad_v[:, None, None].astype(jnp.bfloat16),
    )


def solution(mesh):
    return jax.shard_map(
        body,
        mesh=mesh,
        in_specs=(
            P("head", "tm", "space", None, None, None),
            P("head", "tm", "space", None, None, None),
            P("head", "tm", "space", None, None, None),
            P("head", "tm", "space", None, None, None),
            P("head", "tm", "space", None, None, None),
            P("head", "tm", "space", None, None),
        ),
        out_specs=(
            P("head", "tm", "space", None, None, None),
            P("head", "tm", "space", None, None, None),
            P("head", "tm", "space", None, None, None),
        ),
        check_vma=False,
    )
```

profile of v0, /device:TPU:1, one launch (start us, length us, event | category | flops | bytes accessed | tf_op | source)
XLA Modules:
  0.0 103.0 jit_solution(7057782823995097341)
XLA Ops:
  0.7 2.1 %collective-permute-start.4 = (bf16[2,1,1,1,384,128]{5,4,0,3,2,1:T(8,128)(2,1)}, bf16[2,1,1,1,384,128]{5,4,0,3,2,1:T(8,128)(2,1)S(1)}, u32[]{:S(2)}, u32[]{:S(2)}) collective-permute-start(bf16[2,1,1,1,384,128]{5,4,0,3,2,1:T(8,128)(2,1)} %bitcast.248), channel_id=1, source_target_pairs={{4,0},{8,4},{12,8},{5,1},{9,5},{13,9},{6,2},{10,6},{14,10},{7,3},{... | collective-permute-start | bytes 589832 | tf_op jit(solution)/shard_map/ppermute | solution.py:15
  2.8 4.5 %collective-permute-start.3 = (bf16[2,1,1,1,384,128]{5,4,0,3,2,1:T(8,128)(2,1)}, bf16[2,1,1,1,384,128]{5,4,0,3,2,1:T(8,128)(2,1)S(1)}, u32[]{:S(2)}, u32[]{:S(2)}) collective-permute-start(bf16[2,1,1,1,384,128]{5,4,0,3,2,1:T(8,128)(2,1)} %bitcast.249), channel_id=1, source_target_pairs={{0,4},{4,8},{8,12},{1,5},{5,9},{9,13},{2,6},{6,10},{10,14},{3,7},{... | collective-permute-start | bytes 589832 | tf_op jit(solution)/shard_map/ppermute | solution.py:12
  7.3 1.9 %collective-permute-start.1 = (bf16[2,1,1,1,384,128]{5,4,0,3,2,1:T(8,128)(2,1)}, bf16[2,1,1,1,384,128]{5,4,0,3,2,1:T(8,128)(2,1)S(1)}, u32[]{:S(2)}, u32[]{:S(2)}) collective-permute-start(bf16[2,1,1,1,384,128]{5,4,0,3,2,1:T(8,128)(2,1)} %bitcast.245), channel_id=1, source_target_pairs={{4,0},{8,4},{12,8},{5,1},{9,5},{13,9},{6,2},{10,6},{14,10},{7,3},{... | collective-permute-start | bytes 589832 | tf_op jit(solution)/shard_map/ppermute | solution.py:15
  9.2 3.6 %collective-permute-start = (bf16[2,1,1,1,384,128]{5,4,0,3,2,1:T(8,128)(2,1)}, bf16[2,1,1,1,384,128]{5,4,0,3,2,1:T(8,128)(2,1)S(1)}, u32[]{:S(2)}, u32[]{:S(2)}) collective-permute-start(bf16[2,1,1,1,384,128]{5,4,0,3,2,1:T(8,128)(2,1)} %bitcast.246), channel_id=1, source_target_pairs={{0,4},{4,8},{8,12},{1,5},{5,9},{9,13},{2,6},{6,10},{10,14},{3,7},{... | collective-permute-start | bytes 589832 | tf_op jit(solution)/shard_map/ppermute | solution.py:12
  12.9 0.7 copy.44
  13.5 1.2 %multiply_reduce_fusion = f32[2,384]{1,0:T(2,128)S(1)} fusion(bf16[2,1,1,1,384,128]{5,4,3,2,1,0:T(8,128)(2,1)} %param.81, bf16[2,1,1,1,384,128]{5,4,3,2,1,0:T(8,128)(2,1)} %param.82), kind=kLoop, calls=%fused_computation.131 | loop fusion | flops 392448 | bytes 396288 | tf_op jit(solution)/shard_map/reduce_sum | solution.py:29
  14.8 1.3 %fusion.28 = f32[2,384,384]{2,1,0:T(8,128)S(1)} fusion(f32[]{:T(128)S(6)} %convert_element_type.149, f32[2,384]{1,0:T(2,128)S(1)} %bitcast.251, bf16[2,1,1,1,384,128]{5,4,3,2,1,0:T(8,128)(2,1)} %param.79, bf16[2,1,1,1,384,128]{5,4,3,2,1,0:T(8,128)(2,1)S(1)} %copy-done), kind=kOutput, calls=%fused_computation.49 | convolution fusion | flops 76382208 | bytes 1575940 | tf_op jit(solution)/shard_map/hcqd,hckd->hcqk/dot_general | solution.py:74
  16.4 0.6 copy-done.2
  17.7 0.4 fusion.53
  18.2 1.3 %collective-permute-start.7 = (bf16[2,3,1,1,384,128]{5,4,0,3,2,1:T(8,128)(2,1)S(1)}, bf16[2,3,1,1,384,128]{5,4,0,3,2,1:T(8,128)(2,1)S(1)}, u32[]{:S(2)}, u32[]{:S(2)}) collective-permute-start(bf16[2,3,1,1,384,128]{5,4,0,3,2,1:T(8,128)(2,1)S(1)} %pad_maximum_fusion.3), channel_id=1, source_target_pairs={{1,0},{2,1},{3,2},{5,4},{6,5},{7,6},{9,8},{10,9},{11,10},{13,12},{... | collective-permute-start | bytes 1769480 | tf_op jit(solution)/shard_map/ppermute | solution.py:15
  19.5 4.0 %collective-permute-start.5 = (bf16[2,3,1,1,384,128]{5,4,0,3,2,1:T(8,128)(2,1)S(1)}, bf16[2,3,1,1,384,128]{5,4,0,3,2,1:T(8,128)(2,1)S(1)}, u32[]{:S(2)}, u32[]{:S(2)}) collective-permute-start(bf16[2,3,1,1,384,128]{5,4,0,3,2,1:T(8,128)(2,1)S(1)} %pad_maximum_fusion.3), channel_id=1, source_target_pairs={{0,1},{1,2},{2,3},{4,5},{5,6},{6,7},{8,9},{9,10},{10,11},{12,13},{... | collective-permute-start | bytes 1769480 | tf_op jit(solution)/shard_map/ppermute | solution.py:12
  23.7 1.3 %collective-permute-start.6 = (bf16[2,3,1,1,384,128]{5,4,0,3,2,1:T(8,128)(2,1)S(1)}, bf16[2,3,1,1,384,128]{5,4,0,3,2,1:T(8,128)(2,1)S(1)}, u32[]{:S(2)}, u32[]{:S(2)}) collective-permute-start(bf16[2,3,1,1,384,128]{5,4,0,3,2,1:T(8,128)(2,1)S(1)} %pad_maximum_fusion.2), channel_id=1, source_target_pairs={{1,0},{2,1},{3,2},{5,4},{6,5},{7,6},{9,8},{10,9},{11,10},{13,12},{... | collective-permute-start | bytes 1769480 | tf_op jit(solution)/shard_map/ppermute | solution.py:15
  25.0 4.0 %collective-permute-start.2 = (bf16[2,3,1,1,384,128]{5,4,0,3,2,1:T(8,128)(2,1)S(1)}, bf16[2,3,1,1,384,128]{5,4,0,3,2,1:T(8,128)(2,1)S(1)}, u32[]{:S(2)}, u32[]{:S(2)}) collective-permute-start(bf16[2,3,1,1,384,128]{5,4,0,3,2,1:T(8,128)(2,1)S(1)} %pad_maximum_fusion.2), channel_id=1, source_target_pairs={{0,1},{1,2},{2,3},{4,5},{5,6},{6,7},{8,9},{9,10},{10,11},{12,13},{... | collective-permute-start | bytes 1769480 | tf_op jit(solution)/shard_map/ppermute | solution.py:12
  29.0 0.4 fusion.22
  30.1 0.4 fusion.50
  30.5 0.4 fusion.34
  31.6 0.4 fusion.47
  32.6 16.2 %collective-permute-done.2 = bf16[2,3,1,1,384,128]{5,4,0,3,2,1:T(8,128)(2,1)S(1)} collective-permute-done((bf16[2,3,1,1,384,128]{5,4,0,3,2,1:T(8,128)(2,1)S(1)}, bf16[2,3,1,1,384,128]{5,4,0,3,2,1:T(8,128)(2,1)S(1)}, u32[]{:S(2)}, u32[]{:S(2)}) %collective-permute-start.2) | collective-permute-done | bytes 589856 | tf_op jit(solution)/shard_map/ppermute | solution.py:12
  51.5 0.4 fusion.36
  54.5 1.9 %collective-permute-start.9 = (f32[2,2,3,1,384,128]{5,4,1,0,3,2:T(8,128)S(1)}, f32[2,2,3,1,384,128]{5,4,1,0,3,2:T(8,128)S(1)}, u32[]{:S(2)}, u32[]{:S(2)}) collective-permute-start(f32[2,2,3,1,384,128]{5,4,1,0,3,2:T(8,128)S(1)} %pad_maximum_fusion.1), channel_id=1, source_target_pairs={{0,4},{4,8},{8,12},{1,5},{5,9},{9,13},{2,6},{6,10},{10,14},{3,7},{... | collective-permute-start | bytes 7077896 | tf_op jit(solution)/shard_map/ppermute | solution.py:23
  56.8 2.7 %collective-permute-start.8 = (f32[2,2,3,1,384,128]{5,4,1,0,3,2:T(8,128)S(1)}, f32[2,2,3,1,384,128]{5,4,1,0,3,2:T(8,128)S(1)}, u32[]{:S(2)}, u32[]{:S(2)}) collective-permute-start(f32[2,2,3,1,384,128]{5,4,1,0,3,2:T(8,128)S(1)} %pad_maximum_fusion), channel_id=1, source_target_pairs={{4,0},{8,4},{12,8},{5,1},{9,5},{13,9},{6,2},{10,6},{14,10},{7,3},{... | collective-permute-start | bytes 7077896 | tf_op jit(solution)/shard_map/ppermute | solution.py:23
  59.5 0.4 fusion.26
  62.4 0.4 fusion.126
  63.1 19.1 %collective-permute-done.9 = f32[2,2,3,1,384,128]{5,4,1,0,3,2:T(8,128)S(1)} collective-permute-done((f32[2,2,3,1,384,128]{5,4,1,0,3,2:T(8,128)S(1)}, f32[2,2,3,1,384,128]{5,4,1,0,3,2:T(8,128)S(1)}, u32[]{:S(2)}, u32[]{:S(2)}) %collective-permute-start.9) | collective-permute-done | bytes 2359328 | tf_op jit(solution)/shard_map/ppermute | solution.py:23
  82.2 4.7 %collective-permute-done.8 = f32[2,2,3,1,384,128]{5,4,1,0,3,2:T(8,128)S(1)} collective-permute-done((f32[2,2,3,1,384,128]{5,4,1,0,3,2:T(8,128)S(1)}, f32[2,2,3,1,384,128]{5,4,1,0,3,2:T(8,128)S(1)}, u32[]{:S(2)}, u32[]{:S(2)}) %collective-permute-start.8) | collective-permute-done | bytes 2359328 | tf_op jit(solution)/shard_map/ppermute | solution.py:23
  87.4 1.3 %collective-permute-start.10 = (f32[2,2,1,384,128]{4,3,1,0,2:T(8,128)S(1)}, f32[2,2,1,384,128]{4,3,1,0,2:T(8,128)S(1)}, u32[]{:S(2)}, u32[]{:S(2)}) collective-permute-start(f32[2,2,1,384,128]{4,3,1,0,2:T(8,128)S(1)} %get-tuple-element.366), channel_id=1, source_target_pairs={{1,0},{2,1},{3,2},{5,4},{6,5},{7,6},{9,8},{10,9},{11,10},{13,12},{... | collective-permute-start | bytes 2359304 | tf_op jit(solution)/shard_map/ppermute | solution.py:23
  88.7 4.5 %collective-permute-start.11 = (f32[2,2,1,384,128]{4,3,1,0,2:T(8,128)S(1)}, f32[2,2,1,384,128]{4,3,1,0,2:T(8,128)S(1)}, u32[]{:S(2)}, u32[]{:S(2)}) collective-permute-start(f32[2,2,1,384,128]{4,3,1,0,2:T(8,128)S(1)} %get-tuple-element.367), channel_id=1, source_target_pairs={{0,1},{1,2},{2,3},{4,5},{5,6},{6,7},{8,9},{9,10},{10,11},{12,13},{... | collective-permute-start | bytes 2359304 | tf_op jit(solution)/shard_map/ppermute | solution.py:23
  94.0 0.4 fusion.61
  94.4 1.1 %fusion.63 = bf16[2,1,1,1,384,128]{5,4,3,2,1,0:T(8,128)(2,1)} fusion(f32[2,384,128]{2,1,0:T(8,128)S(1)} %fusion.127, f32[2,384,128]{2,1,0:T(8,128)S(1)} %fusion.77, f32[2,384,128]{2,1,0:T(8,128)S(1)} %fusion.126, f32[2,384,128]{2,1,0:T(8,128)S(1)} %fusion.61, bf16[2,384,384]{2,1,0:T(8,128)(2,1)S(1)} %fusion.42, ...), kind=kOutput, calls=%fused_computation.104 | convolution fusion | flops 76087296 | bytes 2555904 | tf_op jit(solution)/shard_map/hcqk,hckd->hcqd/dot_general | solution.py:87
  95.4 5.2 %collective-permute-done.10 = f32[2,2,1,384,128]{4,3,1,0,2:T(8,128)S(1)} collective-permute-done((f32[2,2,1,384,128]{4,3,1,0,2:T(8,128)S(1)}, f32[2,2,1,384,128]{4,3,1,0,2:T(8,128)S(1)}, u32[]{:S(2)}, u32[]{:S(2)}) %collective-permute-start.10) | collective-permute-done | bytes 786464 | tf_op jit(solution)/shard_map/ppermute | solution.py:23
  100.6 1.5 %collective-permute-done.11 = f32[2,2,1,384,128]{4,3,1,0,2:T(8,128)S(1)} collective-permute-done((f32[2,2,1,384,128]{4,3,1,0,2:T(8,128)S(1)}, f32[2,2,1,384,128]{4,3,1,0,2:T(8,128)S(1)}, u32[]{:S(2)}, u32[]{:S(2)}) %collective-permute-start.11) | collective-permute-done | bytes 786464 | tf_op jit(solution)/shard_map/ppermute | solution.py:23
  102.2 0.8 slice_bitcast_fusion.3
  (61 shorter events, 12.7 us)
Async XLA Ops:
  0.6 14.1 %copy-start = (bf16[2,1,1,1,384,128]{5,4,3,2,1,0:T(8,128)(2,1)S(1)}, bf16[2,1,1,1,384,128]{5,4,3,2,1,0:T(8,128)(2,1)}, u32[]{:S(2)}) copy-start(bf16[2,1,1,1,384,128]{5,4,3,2,1,0:T(8,128)(2,1)} %param.78) | copy-start | bytes 589828
  0.6 15.4 %copy-start.3 = (bf16[2,1,1,1,384,128]{5,4,3,2,1,0:T(8,128)(2,1)S(1)}, bf16[2,1,1,1,384,128]{5,4,3,2,1,0:T(8,128)(2,1)}, u32[]{:S(2)}) copy-start(bf16[2,1,1,1,384,128]{5,4,3,2,1,0:T(8,128)(2,1)} %param.80) | copy-start | bytes 589828
  0.7 15.4 %copy-start.1 = (bf16[2,1,1,1,384,128]{5,4,3,2,1,0:T(8,128)(2,1)S(1)}, bf16[2,1,1,1,384,128]{5,4,3,2,1,0:T(8,128)(2,1)}, u32[]{:S(2)}) copy-start(bf16[2,1,1,1,384,128]{5,4,3,2,1,0:T(8,128)(2,1)} %param.82) | copy-start | bytes 589828
  0.7 17.5 %collective-permute-start.4 = (bf16[2,1,1,1,384,128]{5,4,0,3,2,1:T(8,128)(2,1)}, bf16[2,1,1,1,384,128]{5,4,0,3,2,1:T(8,128)(2,1)S(1)}, u32[]{:S(2)}, u32[]{:S(2)}) collective-permute-start(bf16[2,1,1,1,384,128]{5,4,0,3,2,1:T(8,128)(2,1)} %bitcast.248), channel_id=1, source_target_pairs={{4,0},{8,4},{12,8},{5,1},{9,5},{13,9},{6,2},{10,6},{14,10},{7,3},{... | collective-permute-start | bytes 589832 | tf_op jit(solution)/shard_map/ppermute | solution.py:15
  2.8 15.4 %collective-permute-start.3 = (bf16[2,1,1,1,384,128]{5,4,0,3,2,1:T(8,128)(2,1)}, bf16[2,1,1,1,384,128]{5,4,0,3,2,1:T(8,128)(2,1)S(1)}, u32[]{:S(2)}, u32[]{:S(2)}) collective-permute-start(bf16[2,1,1,1,384,128]{5,4,0,3,2,1:T(8,128)(2,1)} %bitcast.249), channel_id=1, source_target_pairs={{0,4},{4,8},{8,12},{1,5},{5,9},{9,13},{2,6},{6,10},{10,14},{3,7},{... | collective-permute-start | bytes 589832 | tf_op jit(solution)/shard_map/ppermute | solution.py:12
  7.3 16.3 %collective-permute-start.1 = (bf16[2,1,1,1,384,128]{5,4,0,3,2,1:T(8,128)(2,1)}, bf16[2,1,1,1,384,128]{5,4,0,3,2,1:T(8,128)(2,1)S(1)}, u32[]{:S(2)}, u32[]{:S(2)}) collective-permute-start(bf16[2,1,1,1,384,128]{5,4,0,3,2,1:T(8,128)(2,1)} %bitcast.245), channel_id=1, source_target_pairs={{4,0},{8,4},{12,8},{5,1},{9,5},{13,9},{6,2},{10,6},{14,10},{7,3},{... | collective-permute-start | bytes 589832 | tf_op jit(solution)/shard_map/ppermute | solution.py:15
  9.2 14.4 %collective-permute-start = (bf16[2,1,1,1,384,128]{5,4,0,3,2,1:T(8,128)(2,1)}, bf16[2,1,1,1,384,128]{5,4,0,3,2,1:T(8,128)(2,1)S(1)}, u32[]{:S(2)}, u32[]{:S(2)}) collective-permute-start(bf16[2,1,1,1,384,128]{5,4,0,3,2,1:T(8,128)(2,1)} %bitcast.246), channel_id=1, source_target_pairs={{0,4},{4,8},{8,12},{1,5},{5,9},{9,13},{2,6},{6,10},{10,14},{3,7},{... | collective-permute-start | bytes 589832 | tf_op jit(solution)/shard_map/ppermute | solution.py:12
  16.1 0.9 copy-start.2
  18.2 33.9 %collective-permute-start.7 = (bf16[2,3,1,1,384,128]{5,4,0,3,2,1:T(8,128)(2,1)S(1)}, bf16[2,3,1,1,384,128]{5,4,0,3,2,1:T(8,128)(2,1)S(1)}, u32[]{:S(2)}, u32[]{:S(2)}) collective-permute-start(bf16[2,3,1,1,384,128]{5,4,0,3,2,1:T(8,128)(2,1)S(1)} %pad_maximum_fusion.3), channel_id=1, source_target_pairs={{1,0},{2,1},{3,2},{5,4},{6,5},{7,6},{9,8},{10,9},{11,10},{13,12},{... | collective-permute-start | bytes 1769480 | tf_op jit(solution)/shard_map/ppermute | solution.py:15
  19.5 30.7 %collective-permute-start.5 = (bf16[2,3,1,1,384,128]{5,4,0,3,2,1:T(8,128)(2,1)S(1)}, bf16[2,3,1,1,384,128]{5,4,0,3,2,1:T(8,128)(2,1)S(1)}, u32[]{:S(2)}, u32[]{:S(2)}) collective-permute-start(bf16[2,3,1,1,384,128]{5,4,0,3,2,1:T(8,128)(2,1)S(1)} %pad_maximum_fusion.3), channel_id=1, source_target_pairs={{0,1},{1,2},{2,3},{4,5},{5,6},{6,7},{8,9},{9,10},{10,11},{12,13},{... | collective-permute-start | bytes 1769480 | tf_op jit(solution)/shard_map/ppermute | solution.py:12
  23.7 27.8 %collective-permute-start.6 = (bf16[2,3,1,1,384,128]{5,4,0,3,2,1:T(8,128)(2,1)S(1)}, bf16[2,3,1,1,384,128]{5,4,0,3,2,1:T(8,128)(2,1)S(1)}, u32[]{:S(2)}, u32[]{:S(2)}) collective-permute-start(bf16[2,3,1,1,384,128]{5,4,0,3,2,1:T(8,128)(2,1)S(1)} %pad_maximum_fusion.2), channel_id=1, source_target_pairs={{1,0},{2,1},{3,2},{5,4},{6,5},{7,6},{9,8},{10,9},{11,10},{13,12},{... | collective-permute-start | bytes 1769480 | tf_op jit(solution)/shard_map/ppermute | solution.py:15
  25.0 23.9 %collective-permute-start.2 = (bf16[2,3,1,1,384,128]{5,4,0,3,2,1:T(8,128)(2,1)S(1)}, bf16[2,3,1,1,384,128]{5,4,0,3,2,1:T(8,128)(2,1)S(1)}, u32[]{:S(2)}, u32[]{:S(2)}) collective-permute-start(bf16[2,3,1,1,384,128]{5,4,0,3,2,1:T(8,128)(2,1)S(1)} %pad_maximum_fusion.2), channel_id=1, source_target_pairs={{0,1},{1,2},{2,3},{4,5},{5,6},{6,7},{8,9},{9,10},{10,11},{12,13},{... | collective-permute-start | bytes 1769480 | tf_op jit(solution)/shard_map/ppermute | solution.py:12
  54.5 27.7 %collective-permute-start.9 = (f32[2,2,3,1,384,128]{5,4,1,0,3,2:T(8,128)S(1)}, f32[2,2,3,1,384,128]{5,4,1,0,3,2:T(8,128)S(1)}, u32[]{:S(2)}, u32[]{:S(2)}) collective-permute-start(f32[2,2,3,1,384,128]{5,4,1,0,3,2:T(8,128)S(1)} %pad_maximum_fusion.1), channel_id=1, source_target_pairs={{0,4},{4,8},{8,12},{1,5},{5,9},{9,13},{2,6},{6,10},{10,14},{3,7},{... | collective-permute-start | bytes 7077896 | tf_op jit(solution)/shard_map/ppermute | solution.py:23
  56.8 30.2 %collective-permute-start.8 = (f32[2,2,3,1,384,128]{5,4,1,0,3,2:T(8,128)S(1)}, f32[2,2,3,1,384,128]{5,4,1,0,3,2:T(8,128)S(1)}, u32[]{:S(2)}, u32[]{:S(2)}) collective-permute-start(f32[2,2,3,1,384,128]{5,4,1,0,3,2:T(8,128)S(1)} %pad_maximum_fusion), channel_id=1, source_target_pairs={{4,0},{8,4},{12,8},{5,1},{9,5},{13,9},{6,2},{10,6},{14,10},{7,3},{... | collective-permute-start | bytes 7077896 | tf_op jit(solution)/shard_map/ppermute | solution.py:23
  87.4 13.2 %collective-permute-start.10 = (f32[2,2,1,384,128]{4,3,1,0,2:T(8,128)S(1)}, f32[2,2,1,384,128]{4,3,1,0,2:T(8,128)S(1)}, u32[]{:S(2)}, u32[]{:S(2)}) collective-permute-start(f32[2,2,1,384,128]{4,3,1,0,2:T(8,128)S(1)} %get-tuple-element.366), channel_id=1, source_target_pairs={{1,0},{2,1},{3,2},{5,4},{6,5},{7,6},{9,8},{10,9},{11,10},{13,12},{... | collective-permute-start | bytes 2359304 | tf_op jit(solution)/shard_map/ppermute | solution.py:23
  88.7 13.4 %collective-permute-start.11 = (f32[2,2,1,384,128]{4,3,1,0,2:T(8,128)S(1)}, f32[2,2,1,384,128]{4,3,1,0,2:T(8,128)S(1)}, u32[]{:S(2)}, u32[]{:S(2)}) collective-permute-start(f32[2,2,1,384,128]{4,3,1,0,2:T(8,128)S(1)} %get-tuple-element.367), channel_id=1, source_target_pairs={{0,1},{1,2},{2,3},{4,5},{5,6},{6,7},{8,9},{9,10},{10,11},{12,13},{... | collective-permute-start | bytes 2359304 | tf_op jit(solution)/shard_map/ppermute | solution.py:23
where the time goes:
time: 103 us
  waiting for transfers between devices  46.7 us (45%)
  starting transfers between devices  33.2 us (32%)
  matrix products  16.9 us (16%)
  other arithmetic  2.64 us (3%)
  local copies, waits for them, and re-layouts  2.17 us (2%)
  between operations  1.31 us (1%)
    ppermute x4, waiting for transfers between devices, shifted(): return lax.ppermute(value, axis, pairs)  30.5 us
    ppermute x4, waiting for transfers between devices, extended(): lax.ppermute(lax.slice_in_dim(block, block.shape[dim] - width, None, axis...  16.3 us
    ppermute x4, starting transfers between devices, extended(): lax.ppermute(lax.slice_in_dim(block, block.shape[dim] - width, None, axis...  16.2 us
    ppermute x4, starting transfers between devices, shifted(): return lax.ppermute(value, axis, pairs)  10.4 us
    ppermute x4, starting transfers between devices, extended(): lax.ppermute(lax.slice_in_dim(block, 0, width, axis=dim), axis, backward)  6.6 us
    dot_general x9, matrix products, body(): jnp.einsum('hcqd,hckd->hcqk', local_query, key_part, preferred_element_ty...  4.28 us
    dot_general x9, matrix products, body(): jnp.einsum('hcqk,hckd->hcqd', dscore_round, key_part, preferred_element_t...  3.85 us
    dot_general x9, matrix products, body(): jnp.einsum('hcqk,hcqd->hckd', dscore_round, local_query, preferred_elemen...  2.95 us
  transfers between devices with their start and end apart: 12, of which 5 were waited for; matrix products, arithmetic and copies ran while one was open for 17% of the time, Pallas kernels for 0%

commit v1 on v0

v1 whole, which is shorter than its diff:
```python
import functools
import math

import jax
import jax.numpy as jnp
from jax import lax
from jax.experimental import pallas as pl
from jax.experimental.pallas import tpu as pltpu
from jax.sharding import PartitionSpec as P


MESH = pl.DeviceIdType.MESH
LOG2E = math.log2(math.e)
NT_DIMS = (((1,), (1,)), ((), ()))


def member(role, group):
    return 2 * group + lax.rem(role + group, 2)


def kernel(
    rows,
    q_ref, k_ref, v_ref, o_ref, g_ref, lse_ref,
    gq_ref, gk_ref, gv_ref,
    qbuf, gbuf, stat, kbuf, vbuf, kt, own_g, own_o, own_lse, own_stat,
    dq_acc, dk_acc, dv_acc, dq_send, dk_send, dv_send, dq_recv, dk_recv, dv_recv,
    lsem, s_own, s_near, s_cross, s_dq, s_dkv, r_q, r_kv, r_dq, r_dkv,
):
    tile, dim = q_ref.shape[1:]
    scale = dim ** -0.5
    t = lax.axis_index("tm")
    z = lax.axis_index("space")
    group = t // 2
    r = lax.rem(t + group, 2)
    other = 1 - r
    partner = member(other, group)
    has_low = z > 0
    has_high = z < rows - 1
    inner_there = member(1, 1 - group)

    def copy(src, dst, ssem, rsem, tm, space):
        return pltpu.make_async_remote_copy(
            src_ref=src, dst_ref=dst, send_sem=ssem, recv_sem=rsem,
            device_id={"tm": tm, "space": space}, device_id_type=MESH,
        )

    barrier = pltpu.get_barrier_semaphore()

    def greet(tm, space):
        pl.semaphore_signal(
            barrier, inc=1, device_id={"tm": tm, "space": space}, device_id_type=MESH
        )

    greet(partner, z)
    greet(inner_there, z)

    @pl.when(r == 1)
    def _():
        greet(member(0, 1 - group), z)

    @pl.when(has_low)
    def _():
        greet(t, z - 1)
        greet(partner, z - 1)

    @pl.when(has_high)
    def _():
        greet(t, z + 1)
        greet(partner, z + 1)

    local = [
        pltpu.make_async_copy(q_ref.at[r], qbuf.at[r], lsem.at[0]),
        pltpu.make_async_copy(k_ref.at[r], kbuf.at[r], lsem.at[1]),
        pltpu.make_async_copy(v_ref.at[r], vbuf.at[r], lsem.at[2]),
        pltpu.make_async_copy(g_ref.at[r], gbuf.at[r], lsem.at[3]),
        pltpu.make_async_copy(g_ref, own_g, lsem.at[4]),
        pltpu.make_async_copy(o_ref, own_o, lsem.at[5]),
        pltpu.make_async_copy(lse_ref, own_lse, lsem.at[6]),
    ]
    for c in local:
        c.start()

    low_n = has_low.astype(jnp.int32)
    high_n = has_high.astype(jnp.int32)
    pl.semaphore_wait(barrier, 2 + r + 2 * low_n + 2 * high_n)

    def near_copies(direction, k):
        head = r if k == 0 else other
        space = z + 1 if direction == 0 else z - 1
        tm = t if k == 0 else partner
        slot = 2 * (1 + direction) + r
        return [
            copy(src, dst.at[slot], s_near.at[direction, k, i], r_q.at[slot, i], tm, space)
            for i, (src, dst) in enumerate(
                ((q_ref.at[head], qbuf), (g_ref.at[head], gbuf), (own_stat.at[head], stat))
            )
        ]

    own_copies = [
        copy(q_ref.at[other], qbuf.at[r], s_own.at[0], r_q.at[r, 0], partner, z),
        copy(k_ref.at[other], kbuf.at[r], s_own.at[1], r_kv.at[r, 0], partner, z),
        copy(v_ref.at[other], vbuf.at[r], s_own.at[2], r_kv.at[r, 1], partner, z),
        copy(g_ref.at[other], gbuf.at[r], s_own.at[3], r_q.at[r, 1], partner, z),
        copy(own_stat.at[other], stat.at[r], s_own.at[4], r_q.at[r, 2], partner, z),
    ]

    def cross_copies():
        out = []
        for head in range(2):
            tm = member(head, 1 - group)
            out.append(copy(k_ref.at[head], kbuf.at[2], s_cross.at[head, 0], r_kv.at[2, 0], tm, z))
            out.append(copy(v_ref.at[head], vbuf.at[2], s_cross.at[head, 1], r_kv.at[2, 1], tm, z))
        return out

    for k in range(2):
        @pl.when(has_high)
        def _():
            for c in near_copies(0, k)[:2]:
                c.start()

        @pl.when(has_low)
        def _():
            for c in near_copies(1, k)[:2]:
                c.start()

        if k == 0:
            for c in own_copies[:4]:
                c.start()

            @pl.when(r == 1)
            def _():
                for c in cross_copies():
                    c.start()

    for c in local:
        c.wait()
    for head in range(2):
        prod = own_g[head].astype(jnp.float32) * own_o[head].astype(jnp.float32)
        own_stat[head, 0:1, :] = own_lse[head, 0, 0] * LOG2E
        own_stat[head, 1:2, :] = jnp.sum(prod.T, axis=0, keepdims=True)
    own_copies[4].start()
    for k in range(2):
        @pl.when(has_high)
        def _():
            near_copies(0, k)[2].start()

        @pl.when(has_low)
        def _():
            near_copies(1, k)[2].start()

    dq_acc[...] = jnp.zeros_like(dq_acc)
    dk_acc[...] = jnp.zeros_like(dk_acc)
    dv_acc[...] = jnp.zeros_like(dv_acc)
    stat[r] = own_stat[r]
    kt[r] = kbuf[r].T

    def pair(qs, ks):
        qb = qbuf[qs]
        gb = gbuf[qs]
        kb = kbuf[ks]
        vb = vbuf[ks]
        s = lax.dot_general(kb, qb, NT_DIMS, preferred_element_type=jnp.float32)
        p = jnp.exp2(s * (scale * LOG2E) - stat[qs, 0:1, :])
        dp = lax.dot_general(vb, gb, NT_DIMS, preferred_element_type=jnp.float32)
        ds = (p * (dp - stat[qs, 1:2, :])).astype(jnp.bfloat16)
        p = p.astype(jnp.bfloat16)
        dv_acc[ks] += jnp.dot(p, gb, preferred_element_type=jnp.float32)
        dk_acc[ks] += jnp.dot(ds, qb, preferred_element_type=jnp.float32)
        dq_acc[qs] += jnp.dot(kt[ks], ds, preferred_element_type=jnp.float32)

    def q_arrivals(slot):
        return [
            copy(q_ref.at[0], qbuf.at[slot], s_own.at[0], r_q.at[slot, 0], partner, z),
            copy(g_ref.at[0], gbuf.at[slot], s_own.at[0], r_q.at[slot, 1], partner, z),
            copy(own_stat.at[0], stat.at[slot], s_own.at[0], r_q.at[slot, 2], partner, z),
        ]

    def kv_arrivals(slot):
        return [
            copy(k_ref.at[0], kbuf.at[slot], s_own.at[0], r_kv.at[slot, 0], partner, z),
            copy(v_ref.at[0], vbuf.at[slot], s_own.at[0], r_kv.at[slot, 1], partner, z),
        ]

    @pl.loop(0, 4)
    def _(i):
        @pl.when(i == 1)
        def _():
            for c in q_arrivals(other) + kv_arrivals(other):
                c.wait_recv()
            kt[other] = kbuf[other].T

        pair(lax.rem(r + i // 2, 2), lax.rem(r + i, 2))

    for c in kv_arrivals(2):
        c.wait_recv()
    kt[2] = kbuf[2].T

    def dq_copy(slot, source, tm, space):
        return copy(
            dq_send.at[slot], dq_recv.at[r, source], s_dq.at[slot], r_dq.at[r, source], tm, space
        )

    def own_dq_copy():
        return dq_copy(other, 0, partner, z)

    def near_dq_copy(direction, role):
        space = z - 1 if direction == 0 else z + 1
        return dq_copy(2 * (1 + direction) + role, 2 - direction, member(role, group), space)

    def cross_dkv():
        return [
            copy(dk_send.at[2], dk_recv.at[r, 1], s_dkv.at[2, 0], r_dkv.at[r, 1, 0], inner_there, z),
            copy(dv_send.at[2], dv_recv.at[r, 1], s_dkv.at[2, 1], r_dkv.at[r, 1, 1], inner_there, z),
        ]

    def own_dkv():
        return [
            copy(dk_send.at[other], dk_recv.at[r, 0], s_dkv.at[other, 0], r_dkv.at[r, 0, 0], partner, z),
            copy(dv_send.at[other], dv_recv.at[r, 0], s_dkv.at[other, 1], r_dkv.at[r, 0, 1], partner, z),
        ]

    pair(1, 2)

    dq_send[other] = (dq_acc[other] * scale).astype(jnp.bfloat16)
    own_dq_copy().start()

    first = 1 - low_n
    last = 1 + high_n

    @pl.loop(0, 2)
    def _(step):
        role = lax.rem(r + step, 2)

        @pl.when(has_low)
        def _():
            for c in q_arrivals(2 + role):
                c.wait_recv()

        @pl.when(has_high)
        def _():
            for c in q_arrivals(4 + role):
                c.wait_recv()

        @pl.when(role == 1)
        def _():
            @pl.loop(first, last)
            def _(d):
                pair(2 * (1 + d) + 1, 2)

            dk_send[2] = (dk_acc[2] * scale).astype(jnp.bfloat16)
            dv_send[2] = dv_acc[2].astype(jnp.bfloat16)
            for c in cross_dkv():
                c.start()

        @pl.loop(2 * first, 2 * last)
        def _(i):
            d = i // 2
            slot = 2 * (1 + d) + role
            pair(slot, lax.rem(i, 2))

            @pl.when(lax.rem(i, 2) == 1)
            def _():
                dq_send[slot] = (dq_acc[slot] * scale).astype(jnp.bfloat16)

                @pl.when(d == 0)
                def _():
                    near_dq_copy(0, role).start()

                @pl.when(d == 1)
                def _():
                    near_dq_copy(1, role).start()

    dk_send[other] = (dk_acc[other] * scale).astype(jnp.bfloat16)
    dv_send[other] = dv_acc[other].astype(jnp.bfloat16)
    for c in own_dkv():
        c.start()

    def dq_arrival(head, source):
        return copy(
            dq_send.at[0], dq_recv.at[head, source], s_own.at[0], r_dq.at[head, source], partner, z
        )

    def dkv_arrivals(head, source):
        return [
            copy(dk_send.at[0], dk_recv.at[head, source], s_own.at[0], r_dkv.at[head, source, 0], partner, z),
            copy(dv_send.at[0], dv_recv.at[head, source], s_own.at[0], r_dkv.at[head, source, 1], partner, z),
        ]

    dk_mine = dk_acc[r] * scale
    dv_mine = dv_acc[r]

    @pl.when(r == 0)
    def _():
        gk_ref[r] = dk_mine.astype(gk_ref.dtype)
        gv_ref[r] = dv_mine.astype(gv_ref.dtype)
        for c in dkv_arrivals(other, 0):
            c.wait_recv()
        gk_ref[other] = dk_recv[other, 0]
        gv_ref[other] = dv_recv[other, 0]

    @pl.when(r == 1)
    def _():
        for c in dkv_arrivals(0, 1) + dkv_arrivals(1, 1):
            c.wait_recv()
        gk_ref[r] = (dk_mine + dk_recv[r, 1].astype(jnp.float32)).astype(gk_ref.dtype)
        gv_ref[r] = (dv_mine + dv_recv[r, 1].astype(jnp.float32)).astype(gv_ref.dtype)
        for c in dkv_arrivals(other, 0):
            c.wait_recv()
        for recv, out in ((dk_recv, gk_ref), (dv_recv, gv_ref)):
            out[other] = (
                recv[other, 0].astype(jnp.float32) + recv[other, 1].astype(jnp.float32)
            ).astype(out.dtype)

    dq_arrival(other, 0).wait_recv()
    totals = [dq_acc.at[r], dq_acc.at[other]]
    dq_acc[r] = dq_acc[r] * scale
    dq_acc[other] = dq_recv[other, 0].astype(jnp.float32)

    for source, there in ((1, has_low), (2, has_high)):
        @pl.when(there)
        def _():
            for head, total in ((r, totals[0]), (other, totals[1])):
                dq_arrival(head, source).wait_recv()
                total[...] += dq_recv[head, source].astype(jnp.float32)

    for head, total in ((r, totals[0]), (other, totals[1])):
        gq_ref[head] = total[...].T.astype(gq_ref.dtype)

    for c in own_copies + [own_dq_copy()] + cross_dkv() + own_dkv():
        c.wait_send()

    @pl.when(r == 1)
    def _():
        for c in cross_copies():
            c.wait_send()

    @pl.when(has_high)
    def _():
        for c in near_copies(0, 0) + near_copies(0, 1):
            c.wait_send()
        for role in range(2):
            near_dq_copy(1, role).wait_send()

    @pl.when(has_low)
    def _():
        for c in near_copies(1, 0) + near_copies(1, 1):
            c.wait_send()
        for role in range(2):
            near_dq_copy(0, role).wait_send()


def body(rows, query_tiles, key_tiles, value_tiles, out_tiles, grad_tiles, log_sum_exp):
    heads, _, _, columns, tile, dim = query_tiles.shape
    flat = (heads, tile, dim)
    bf, f32 = jnp.bfloat16, jnp.float32
    dma = pltpu.SemaphoreType.DMA
    outs = pl.pallas_call(
        functools.partial(kernel, rows),
        out_shape=[jax.ShapeDtypeStruct(flat, bf)] * 3,
        in_specs=[pl.BlockSpec(memory_space=pl.ANY)] * 6,
        out_specs=[pl.BlockSpec(memory_space=pltpu.VMEM)] * 3,
        scratch_shapes=[
            pltpu.VMEM((6, tile, dim), bf),
            pltpu.VMEM((6, tile, dim), bf),
            pltpu.VMEM((6, 2, tile), f32),
            pltpu.VMEM((3, tile, dim), bf),
            pltpu.VMEM((3, tile, dim), bf),
            pltpu.VMEM((3, dim, tile), bf),
            pltpu.VMEM(flat, bf),
            pltpu.VMEM(flat, bf),
            pltpu.VMEM((heads, 1, 1, 1, tile), f32),
            pltpu.VMEM((heads, 2, tile), f32),
            pltpu.VMEM((6, dim, tile), f32),
            pltpu.VMEM((3, tile, dim), f32),
            pltpu.VMEM((3, tile, dim), f32),
            pltpu.VMEM((6, dim, tile), bf),
            pltpu.VMEM((3, tile, dim), bf),
            pltpu.VMEM((3, tile, dim), bf),
            pltpu.VMEM((2, 3, dim, tile), bf),
            pltpu.VMEM((2, 2, tile, dim), bf),
            pltpu.VMEM((2, 2, tile, dim), bf),
            dma((7,)),
            dma((5,)),
            dma((2, 2, 3)),
            dma((2, 2)),
            dma((6,)),
            dma((3, 2)),
            dma((6, 3)),
            dma((3, 2)),
            dma((2, 3)),
            dma((2, 2, 2)),
        ],
        compiler_params=pltpu.CompilerParams(
            collective_id=0, has_side_effects=True, vmem_limit_bytes=40 * 2**20
        ),
        cost_estimate=pl.CostEstimate(
            flops=15 * 5 * 2 * tile * tile * dim,
            bytes_accessed=16 * tile * dim * 2,
            transcendentals=15 * tile * tile,
        ),
        name="tile_attention_backward",
    )(
        query_tiles.reshape(flat), key_tiles.reshape(flat), value_tiles.reshape(flat),
        out_tiles.reshape(flat), grad_tiles.reshape(flat), log_sum_exp,
    )
    return tuple(o.reshape(query_tiles.shape) for o in outs)


def solution(mesh):
    tiles = P("head", "tm", "space", None, None, None)
    assert mesh.shape["tm"] == 4
    return jax.shard_map(
        functools.partial(body, mesh.shape["space"]),
        mesh=mesh,
        in_specs=(tiles,) * 5 + (P("head", "tm", "space", None, None),),
        out_specs=(tiles,) * 3,
        check_vma=False,
    )
```

time: 103 us -> 31.3 us (0.30)
  waiting for transfers between devices: 46.7 us -> 0 us
  starting transfers between devices: 33.2 us -> 0 us
  Pallas kernels: 0 us -> 23.1 us
  matrix products: 16.9 us -> 0 us
  local copies, waits for them, and re-layouts: 2.17 us -> 7.34 us
  other arithmetic: 2.64 us -> 0 us
    ppermute x12 -> x0, waiting for transfers between devices: 46.7 us -> none  [the longest x4 30.5 us: shifted(): return lax.ppermute(value, axis, pairs)]
    ppermute x12 -> x0, starting transfers between devices: 33.2 us -> none  [the longest x4 16.2 us: extended(): lax.ppermute(lax.slice_in_dim(block, block.shape[dim] - width, None, axis...]
    pallas_call x0 -> x1, Pallas kernels: none -> 23.1 us  [body(): pl.pallas_call(functools.partial(kernel, rows), out_shape=[jax.ShapeDtype...]
    dot_general x45 -> x0, matrix products: 16.9 us -> none  [the longest x9 4.28 us: body(): jnp.einsum('hcqd,hckd->hcqk', local_query, key_part, preferred_element_ty...]
    unnamed x10 -> x15, local copies, waits for them, and re-layouts: 2.07 us -> 7.34 us
    reduce_sum x1 -> x0, other arithmetic: 1.2 us -> none  [body(): jnp.sum(grad_tiles.astype(jnp.float32) * out_tiles.astype(jnp.float32), a...]
  transfers between devices with their start and end apart: 12 -> 0, of which waited for: 5 -> 0; matrix products, arithmetic and copies ran while one was open for 17% -> 0% of each run, Pallas kernels for 0% -> 0%
where the time goes in v1:
time: 31.3 us; the launch traced here: 31.1 us
  Pallas kernels  23.1 us (74%)
  local copies, waits for them, and re-layouts  7.34 us (23%)
  between operations  0.65 us (2%)
    pallas_call x1, Pallas kernels, body(): pl.pallas_call(functools.partial(kernel, rows), out_shape=[jax.ShapeDtype...  23.1 us
    unnamed x15, local copies, waits for them, and re-layouts  7.34 us

profile of v1, /device:TPU:1, one launch (start us, length us, event | category | flops | bytes accessed | tf_op | source)
XLA Modules:
  0.0 31.1 jit_solution(7150293640288605299)
XLA Ops:
  0.6 0.0 copy-start.5
  0.6 0.7 %copy-done.5 = f32[2,1,1,1,384]{4,3,2,1,0:T(1,128)S(1)} copy-done((f32[2,1,1,1,384]{4,3,2,1,0:T(1,128)S(1)}, f32[2,1,1,1,384]{4,3,2,1,0:T(1,128)}, u32[]{:S(2)}) %copy-start.5) | copy-done | bytes 3096
  1.3 0.0 copy-start
  1.3 0.9 %copy-done = bf16[2,1,1,1,384,128]{5,4,3,2,1,0:T(8,128)(2,1)S(1)} copy-done((bf16[2,1,1,1,384,128]{5,4,3,2,1,0:T(8,128)(2,1)S(1)}, bf16[2,1,1,1,384,128]{5,4,3,2,1,0:T(8,128)(2,1)}, u32[]{:S(2)}) %copy-start) | copy-done | bytes 196632
  2.2 0.0 copy-start.1
  2.2 0.9 %copy-done.1 = bf16[2,1,1,1,384,128]{5,4,3,2,1,0:T(8,128)(2,1)S(1)} copy-done((bf16[2,1,1,1,384,128]{5,4,3,2,1,0:T(8,128)(2,1)S(1)}, bf16[2,1,1,1,384,128]{5,4,3,2,1,0:T(8,128)(2,1)}, u32[]{:S(2)}) %copy-start.1) | copy-done | bytes 196632
  3.2 0.0 copy-start.2
  3.2 0.9 %copy-done.2 = bf16[2,1,1,1,384,128]{5,4,3,2,1,0:T(8,128)(2,1)S(1)} copy-done((bf16[2,1,1,1,384,128]{5,4,3,2,1,0:T(8,128)(2,1)S(1)}, bf16[2,1,1,1,384,128]{5,4,3,2,1,0:T(8,128)(2,1)}, u32[]{:S(2)}) %copy-start.2) | copy-done | bytes 196632
  4.1 0.0 copy-start.3
  4.1 0.9 %copy-done.3 = bf16[2,1,1,1,384,128]{5,4,3,2,1,0:T(8,128)(2,1)S(1)} copy-done((bf16[2,1,1,1,384,128]{5,4,3,2,1,0:T(8,128)(2,1)S(1)}, bf16[2,1,1,1,384,128]{5,4,3,2,1,0:T(8,128)(2,1)}, u32[]{:S(2)}) %copy-start.3) | copy-done | bytes 196632
  5.0 0.0 copy-start.4
  5.0 0.9 %copy-done.4 = bf16[2,1,1,1,384,128]{5,4,3,2,1,0:T(8,128)(2,1)S(1)} copy-done((bf16[2,1,1,1,384,128]{5,4,3,2,1,0:T(8,128)(2,1)S(1)}, bf16[2,1,1,1,384,128]{5,4,3,2,1,0:T(8,128)(2,1)}, u32[]{:S(2)}) %copy-start.4) | copy-done | bytes 196632
  6.0 23.1 %tile_attention_backward.1 = (bf16[2,384,128]{2,1,0:T(8,128)(2,1)S(1)}, bf16[2,384,128]{2,1,0:T(8,128)(2,1)S(1)}, bf16[2,384,128]{2,1,0:T(8,128)(2,1)S(1)}) custom-call(bf16[2,384,128]{2,1,0:T(8,128)(2,1)S(1)} %bitcast.17, bf16[2,384,128]{2,1,0:T(8,128)(2,1)S(1)} %bitcast.18, bf16[2,384,128]{2,1,0:T(8,128)(2,1)S(1)} %bitcast.19, ...), custom_call_target="tpu_custom_call" | custom-call | flops 2831155200 | bytes 1572864 | tf_op jit(solution)/shard_map/tile_attention_backward/pallas_call | solution.py:357
  29.0 0.7 %copy.15 = bf16[2,1,1,1,384,128]{5,4,3,2,1,0:T(8,128)(2,1)} copy(bf16[2,1,1,1,384,128]{5,4,3,2,1,0:T(8,128)(2,1)S(1)} %bitcast.16) | data formatting | bytes 393216
  29.7 0.7 %copy.16 = bf16[2,1,1,1,384,128]{5,4,3,2,1,0:T(8,128)(2,1)} copy(bf16[2,1,1,1,384,128]{5,4,3,2,1,0:T(8,128)(2,1)S(1)} %bitcast.15) | data formatting | bytes 393216
  30.4 0.7 %copy.17 = bf16[2,1,1,1,384,128]{5,4,3,2,1,0:T(8,128)(2,1)} copy(bf16[2,1,1,1,384,128]{5,4,3,2,1,0:T(8,128)(2,1)S(1)} %bitcast.14) | data formatting | bytes 393216
Async XLA Ops:
  0.6 0.7 %copy-start.5 = (f32[2,1,1,1,384]{4,3,2,1,0:T(1,128)S(1)}, f32[2,1,1,1,384]{4,3,2,1,0:T(1,128)}, u32[]{:S(2)}) copy-start(f32[2,1,1,1,384]{4,3,2,1,0:T(1,128)} %lse_ref.1) | copy-start | bytes 9220
  1.3 0.9 %copy-start = (bf16[2,1,1,1,384,128]{5,4,3,2,1,0:T(8,128)(2,1)S(1)}, bf16[2,1,1,1,384,128]{5,4,3,2,1,0:T(8,128)(2,1)}, u32[]{:S(2)}) copy-start(bf16[2,1,1,1,384,128]{5,4,3,2,1,0:T(8,128)(2,1)} %param.6) | copy-start | bytes 589828
  2.2 0.9 %copy-start.1 = (bf16[2,1,1,1,384,128]{5,4,3,2,1,0:T(8,128)(2,1)S(1)}, bf16[2,1,1,1,384,128]{5,4,3,2,1,0:T(8,128)(2,1)}, u32[]{:S(2)}) copy-start(bf16[2,1,1,1,384,128]{5,4,3,2,1,0:T(8,128)(2,1)} %param.7) | copy-start | bytes 589828
  3.2 0.9 %copy-start.2 = (bf16[2,1,1,1,384,128]{5,4,3,2,1,0:T(8,128)(2,1)S(1)}, bf16[2,1,1,1,384,128]{5,4,3,2,1,0:T(8,128)(2,1)}, u32[]{:S(2)}) copy-start(bf16[2,1,1,1,384,128]{5,4,3,2,1,0:T(8,128)(2,1)} %param.8) | copy-start | bytes 589828
  4.1 0.9 %copy-start.3 = (bf16[2,1,1,1,384,128]{5,4,3,2,1,0:T(8,128)(2,1)S(1)}, bf16[2,1,1,1,384,128]{5,4,3,2,1,0:T(8,128)(2,1)}, u32[]{:S(2)}) copy-start(bf16[2,1,1,1,384,128]{5,4,3,2,1,0:T(8,128)(2,1)} %param.9) | copy-start | bytes 589828
  5.0 0.9 %copy-start.4 = (bf16[2,1,1,1,384,128]{5,4,3,2,1,0:T(8,128)(2,1)S(1)}, bf16[2,1,1,1,384,128]{5,4,3,2,1,0:T(8,128)(2,1)}, u32[]{:S(2)}) copy-start(bf16[2,1,1,1,384,128]{5,4,3,2,1,0:T(8,128)(2,1)} %param.10) | copy-start | bytes 589828

commit v2 on v1

--- a/solution.py
+++ b/solution.py
@@ -21,7 +21,7 @@
 def kernel(
     rows,
     q_ref, k_ref, v_ref, o_ref, g_ref, lse_ref,
-    gq_ref, gk_ref, gv_ref,
+    grads_ref,
     qbuf, gbuf, stat, kbuf, vbuf, kt, own_g, own_o, own_lse, own_stat,
     dq_acc, dk_acc, dv_acc, dq_send, dk_send, dv_send, dq_recv, dk_recv, dv_recv,
     lsem, s_own, s_near, s_cross, s_dq, s_dkv, r_q, r_kv, r_dq, r_dkv,
@@ -44,6 +44,7 @@
             device_id={"tm": tm, "space": space}, device_id_type=MESH,
         )
 
+    gq_ref, gk_ref, gv_ref = (grads_ref.at[i] for i in range(3))
     barrier = pltpu.get_barrier_semaphore()
 
     def greet(tm, space):
@@ -84,7 +85,7 @@
     high_n = has_high.astype(jnp.int32)
     pl.semaphore_wait(barrier, 2 + r + 2 * low_n + 2 * high_n)
 
-    def near_copies(direction, k):
+    def near_copies(direction, k, parts=(0, 1, 2)):
         head = r if k == 0 else other
         space = z + 1 if direction == 0 else z - 1
         tm = t if k == 0 else partner
@@ -94,6 +95,7 @@
             for i, (src, dst) in enumerate(
                 ((q_ref.at[head], qbuf), (g_ref.at[head], gbuf), (own_stat.at[head], stat))
             )
+            if i in parts
         ]
 
     own_copies = [
@@ -115,12 +117,12 @@
     for k in range(2):
         @pl.when(has_high)
         def _():
-            for c in near_copies(0, k)[:2]:
+            for c in near_copies(0, k, (0, 1)):
                 c.start()
 
         @pl.when(has_low)
         def _():
-            for c in near_copies(1, k)[:2]:
+            for c in near_copies(1, k, (0, 1)):
                 c.start()
 
         if k == 0:
@@ -142,11 +144,11 @@
     for k in range(2):
         @pl.when(has_high)
         def _():
-            near_copies(0, k)[2].start()
+            near_copies(0, k, (2,))[0].start()
 
         @pl.when(has_low)
         def _():
-            near_copies(1, k)[2].start()
+            near_copies(1, k, (2,))[0].start()
 
     dq_acc[...] = jnp.zeros_like(dq_acc)
     dk_acc[...] = jnp.zeros_like(dk_acc)
@@ -354,11 +356,11 @@
     flat = (heads, tile, dim)
     bf, f32 = jnp.bfloat16, jnp.float32
     dma = pltpu.SemaphoreType.DMA
-    outs = pl.pallas_call(
+    grads = pl.pallas_call(
         functools.partial(kernel, rows),
-        out_shape=[jax.ShapeDtypeStruct(flat, bf)] * 3,
-        in_specs=[pl.BlockSpec(memory_space=pl.ANY)] * 6,
-        out_specs=[pl.BlockSpec(memory_space=pltpu.VMEM)] * 3,
+        out_shape=jax.ShapeDtypeStruct((3,) + flat, bf),
+        in_specs=[pl.BlockSpec(memory_space=pltpu.HBM)] * 6,
+        out_specs=pl.BlockSpec(memory_space=pltpu.VMEM),
         scratch_shapes=[
             pltpu.VMEM((6, tile, dim), bf),
             pltpu.VMEM((6, tile, dim), bf),
@@ -391,7 +393,7 @@
             dma((2, 2, 2)),
         ],
         compiler_params=pltpu.CompilerParams(
-            collective_id=0, has_side_effects=True, vmem_limit_bytes=40 * 2**20
+            collective_id=0, has_side_effects=True, vmem_limit_bytes=60 * 2**20
         ),
         cost_estimate=pl.CostEstimate(
             flops=15 * 5 * 2 * tile * tile * dim,
@@ -403,6 +405,7 @@
         query_tiles.reshape(flat), key_tiles.reshape(flat), value_tiles.reshape(flat),
         out_tiles.reshape(flat), grad_tiles.reshape(flat), log_sum_exp,
     )
+    outs = (grads[0], grads[1], grads[2])
     return tuple(o.reshape(query_tiles.shape) for o in outs)
 
 

time: 31.3 us -> 26.9 us (0.86)
  local copies, waits for them, and re-layouts: 7.34 us -> 1.94 us
  Pallas kernels: 23.1 us -> 24.2 us
    unnamed x15 -> x1, local copies, waits for them, and re-layouts: 7.34 us -> 1.94 us
    pallas_call x1, Pallas kernels: 23.1 us -> 24.2 us  [body(): pl.pallas_call(functools.partial(kernel, rows), out_shape=jax.ShapeDtypeS...]
where the time goes in v2:
time: 26.9 us; the launch traced here: 26.8 us
  Pallas kernels  24.2 us (90%)
  local copies, waits for them, and re-layouts  1.94 us (7%)
  between operations  0.64 us (2%)
    pallas_call x1, Pallas kernels, body(): pl.pallas_call(functools.partial(kernel, rows), out_shape=jax.ShapeDtypeS...  24.2 us
    unnamed x1, local copies, waits for them, and re-layouts  1.94 us

profile of v2, /device:TPU:1, one launch (start us, length us, event | category | flops | bytes accessed | tf_op | source)
XLA Modules:
  0.0 26.8 jit_solution(8346561281852303757)
XLA Ops:
  0.6 24.2 %tile_attention_backward.1 = bf16[3,2,384,128]{3,2,1,0:T(8,128)(2,1)} custom-call(bf16[2,384,128]{2,1,0:T(8,128)(2,1)} %bitcast.17, bf16[2,384,128]{2,1,0:T(8,128)(2,1)} %bitcast.18, bf16[2,384,128]{2,1,0:T(8,128)(2,1)} %bitcast.19, bf16[2,384,128]{2,1,0:T(8,128)(2,1)} %bitcast.20, bf16[2,384,128]{2,1,0:T(8,128)(2,1)} %bitcast.21, f32[2,1,1,1,384]{4,3,2,1,0:T(1,128)} %lse_ref.1), custom_call_target="tpu_custom_call" | custom-call | flops 2831155200 | bytes 1572864 | tf_op jit(solution)/shard_map/tile_attention_backward/pallas_call | solution.py:359
  24.9 1.9 %slice_bitcast_fusion = (bf16[2,1,1,1,384,128]{5,4,3,2,1,0:T(8,128)(2,1)}, bf16[2,1,1,1,384,128]{5,4,3,2,1,0:T(8,128)(2,1)}, bf16[2,1,1,1,384,128]{5,4,3,2,1,0:T(8,128)(2,1)}) fusion(bf16[3,2,384,128]{3,2,1,0:T(8,128)(2,1)} %tile_attention_backward.1), kind=kLoop, calls=%fused_computation | loop fusion | bytes 1179648

commit v3 on v2

--- a/solution.py
+++ b/solution.py
@@ -81,11 +81,18 @@
     for c in local:
         c.start()
 
+    for c in local:
+        c.wait()
+    for head in range(2):
+        prod = own_g[head].astype(jnp.float32) * own_o[head].astype(jnp.float32)
+        own_stat[head, 0:1, :] = own_lse[head, 0, 0] * LOG2E
+        own_stat[head, 1:2, :] = jnp.sum(prod.T, axis=0, keepdims=True)
+
     low_n = has_low.astype(jnp.int32)
     high_n = has_high.astype(jnp.int32)
     pl.semaphore_wait(barrier, 2 + r + 2 * low_n + 2 * high_n)
 
-    def near_copies(direction, k, parts=(0, 1, 2)):
+    def near_copies(direction, k):
         head = r if k == 0 else other
         space = z + 1 if direction == 0 else z - 1
         tm = t if k == 0 else partner
@@ -93,17 +100,16 @@
         return [
             copy(src, dst.at[slot], s_near.at[direction, k, i], r_q.at[slot, i], tm, space)
             for i, (src, dst) in enumerate(
-                ((q_ref.at[head], qbuf), (g_ref.at[head], gbuf), (own_stat.at[head], stat))
+                ((own_stat.at[head], stat), (q_ref.at[head], qbuf), (g_ref.at[head], gbuf))
             )
-            if i in parts
         ]
 
     own_copies = [
-        copy(q_ref.at[other], qbuf.at[r], s_own.at[0], r_q.at[r, 0], partner, z),
-        copy(k_ref.at[other], kbuf.at[r], s_own.at[1], r_kv.at[r, 0], partner, z),
-        copy(v_ref.at[other], vbuf.at[r], s_own.at[2], r_kv.at[r, 1], partner, z),
-        copy(g_ref.at[other], gbuf.at[r], s_own.at[3], r_q.at[r, 1], partner, z),
-        copy(own_stat.at[other], stat.at[r], s_own.at[4], r_q.at[r, 2], partner, z),
+        copy(own_stat.at[other], stat.at[r], s_own.at[0], r_q.at[r, 0], partner, z),
+        copy(q_ref.at[other], qbuf.at[r], s_own.at[1], r_q.at[r, 1], partner, z),
+        copy(k_ref.at[other], kbuf.at[r], s_own.at[2], r_kv.at[r, 0], partner, z),
+        copy(g_ref.at[other], gbuf.at[r], s_own.at[3], r_q.at[r, 2], partner, z),
+        copy(v_ref.at[other], vbuf.at[r], s_own.at[4], r_kv.at[r, 1], partner, z),
     ]
 
     def cross_copies():
@@ -114,41 +120,25 @@
             out.append(copy(v_ref.at[head], vbuf.at[2], s_cross.at[head, 1], r_kv.at[2, 1], tm, z))
         return out
 
+    for c in own_copies:
+        c.start()
+
     for k in range(2):
         @pl.when(has_high)
         def _():
-            for c in near_copies(0, k, (0, 1)):
+            for c in near_copies(0, k):
                 c.start()
 
         @pl.when(has_low)
         def _():
-            for c in near_copies(1, k, (0, 1)):
+            for c in near_copies(1, k):
                 c.start()
 
         if k == 0:
-            for c in own_copies[:4]:
-                c.start()
-
             @pl.when(r == 1)
             def _():
                 for c in cross_copies():
                     c.start()
-
-    for c in local:
-        c.wait()
-    for head in range(2):
-        prod = own_g[head].astype(jnp.float32) * own_o[head].astype(jnp.float32)
-        own_stat[head, 0:1, :] = own_lse[head, 0, 0] * LOG2E
-        own_stat[head, 1:2, :] = jnp.sum(prod.T, axis=0, keepdims=True)
-    own_copies[4].start()
-    for k in range(2):
-        @pl.when(has_high)
-        def _():
-            near_copies(0, k, (2,))[0].start()
-
-        @pl.when(has_low)
-        def _():
-            near_copies(1, k, (2,))[0].start()
 
     dq_acc[...] = jnp.zeros_like(dq_acc)
     dk_acc[...] = jnp.zeros_like(dk_acc)
@@ -172,9 +162,9 @@
 
     def q_arrivals(slot):
         return [
-            copy(q_ref.at[0], qbuf.at[slot], s_own.at[0], r_q.at[slot, 0], partner, z),
-            copy(g_ref.at[0], gbuf.at[slot], s_own.at[0], r_q.at[slot, 1], partner, z),
-            copy(own_stat.at[0], stat.at[slot], s_own.at[0], r_q.at[slot, 2], partner, z),
+            copy(own_stat.at[0], stat.at[slot], s_own.at[0], r_q.at[slot, 0], partner, z),
+            copy(q_ref.at[0], qbuf.at[slot], s_own.at[0], r_q.at[slot, 1], partner, z),
+            copy(g_ref.at[0], gbuf.at[slot], s_own.at[0], r_q.at[slot, 2], partner, z),
         ]
 
     def kv_arrivals(slot):

time: 26.9 us -> 24.2 us (0.90)
  Pallas kernels: 24.2 us -> 21.5 us
    pallas_call x1, Pallas kernels: 24.2 us -> 21.5 us  [body(): pl.pallas_call(functools.partial(kernel, rows), out_shape=jax.ShapeDtypeS...]
where the time goes in v3:
time: 24.2 us; the launch traced here: 24.1 us
  Pallas kernels  21.5 us (89%)
  local copies, waits for them, and re-layouts  1.94 us (8%)
  between operations  0.64 us (3%)
    pallas_call x1, Pallas kernels, body(): pl.pallas_call(functools.partial(kernel, rows), out_shape=jax.ShapeDtypeS...  21.5 us
    unnamed x1, local copies, waits for them, and re-layouts  1.94 us

profile of v3, /device:TPU:1, one launch (start us, length us, event | category | flops | bytes accessed | tf_op | source)
XLA Modules:
  0.0 24.1 jit_solution(5554091797280479888)
XLA Ops:
  0.6 21.5 %tile_attention_backward.1 = bf16[3,2,384,128]{3,2,1,0:T(8,128)(2,1)} custom-call(bf16[2,384,128]{2,1,0:T(8,128)(2,1)} %bitcast.17, bf16[2,384,128]{2,1,0:T(8,128)(2,1)} %bitcast.18, bf16[2,384,128]{2,1,0:T(8,128)(2,1)} %bitcast.19, bf16[2,384,128]{2,1,0:T(8,128)(2,1)} %bitcast.20, bf16[2,384,128]{2,1,0:T(8,128)(2,1)} %bitcast.21, f32[2,1,1,1,384]{4,3,2,1,0:T(1,128)} %lse_ref.1), custom_call_target="tpu_custom_call" | custom-call | flops 2831155200 | bytes 1572864 | tf_op jit(solution)/shard_map/tile_attention_backward/pallas_call | solution.py:349
  22.1 1.9 %slice_bitcast_fusion = (bf16[2,1,1,1,384,128]{5,4,3,2,1,0:T(8,128)(2,1)}, bf16[2,1,1,1,384,128]{5,4,3,2,1,0:T(8,128)(2,1)}, bf16[2,1,1,1,384,128]{5,4,3,2,1,0:T(8,128)(2,1)}) fusion(bf16[3,2,384,128]{3,2,1,0:T(8,128)(2,1)} %tile_attention_backward.1), kind=kLoop, calls=%fused_computation | loop fusion | bytes 1179648

commit v4 on v3

--- a/solution.py
+++ b/solution.py
@@ -22,9 +22,9 @@
     rows,
     q_ref, k_ref, v_ref, o_ref, g_ref, lse_ref,
     grads_ref,
-    qbuf, gbuf, stat, kbuf, vbuf, kt, own_g, own_o, own_lse, own_stat,
+    grads, qbuf, gbuf, stat, kbuf, vbuf, kt, own_g, own_o, own_lse, own_stat,
     dq_acc, dk_acc, dv_acc, dq_send, dk_send, dv_send, dq_recv, dk_recv, dv_recv,
-    lsem, s_own, s_near, s_cross, s_dq, s_dkv, r_q, r_kv, r_dq, r_dkv,
+    lsem, s_own, s_near, s_cross, s_dq, s_dkv, r_q, r_kv, r_dq, r_dkv, w_out,
 ):
     tile, dim = q_ref.shape[1:]
     scale = dim ** -0.5
@@ -44,7 +44,7 @@
             device_id={"tm": tm, "space": space}, device_id_type=MESH,
         )
 
-    gq_ref, gk_ref, gv_ref = (grads_ref.at[i] for i in range(3))
+    gq_ref, gk_ref, gv_ref = (grads.at[i] for i in range(3))
     barrier = pltpu.get_barrier_semaphore()
 
     def greet(tm, space):
@@ -278,6 +278,9 @@
             copy(dv_send.at[0], dv_recv.at[head, source], s_own.at[0], r_dkv.at[head, source, 1], partner, z),
         ]
 
+    def write(i, head):
+        return pltpu.make_async_copy(grads.at[i, head], grads_ref.at[i, head], w_out.at[i, head])
+
     dk_mine = dk_acc[r] * scale
     dv_mine = dv_acc[r]
 
@@ -285,10 +288,14 @@
     def _():
         gk_ref[r] = dk_mine.astype(gk_ref.dtype)
         gv_ref[r] = dv_mine.astype(gv_ref.dtype)
+        write(1, r).start()
+        write(2, r).start()
         for c in dkv_arrivals(other, 0):
             c.wait_recv()
         gk_ref[other] = dk_recv[other, 0]
         gv_ref[other] = dv_recv[other, 0]
+        write(1, other).start()
+        write(2, other).start()
 
     @pl.when(r == 1)
     def _():
@@ -296,12 +303,16 @@
             c.wait_recv()
         gk_ref[r] = (dk_mine + dk_recv[r, 1].astype(jnp.float32)).astype(gk_ref.dtype)
         gv_ref[r] = (dv_mine + dv_recv[r, 1].astype(jnp.float32)).astype(gv_ref.dtype)
+        write(1, r).start()
+        write(2, r).start()
         for c in dkv_arrivals(other, 0):
             c.wait_recv()
         for recv, out in ((dk_recv, gk_ref), (dv_recv, gv_ref)):
             out[other] = (
                 recv[other, 0].astype(jnp.float32) + recv[other, 1].astype(jnp.float32)
             ).astype(out.dtype)
+        write(1, other).start()
+        write(2, other).start()
 
     dq_arrival(other, 0).wait_recv()
     totals = [dq_acc.at[r], dq_acc.at[other]]
@@ -317,6 +328,7 @@
 
     for head, total in ((r, totals[0]), (other, totals[1])):
         gq_ref[head] = total[...].T.astype(gq_ref.dtype)
+        write(0, head).start()
 
     for c in own_copies + [own_dq_copy()] + cross_dkv() + own_dkv():
         c.wait_send()
@@ -339,6 +351,10 @@
             c.wait_send()
         for role in range(2):
             near_dq_copy(0, role).wait_send()
+
+    for i in range(3):
+        for head in range(2):
+            write(i, head).wait()
 
 
 def body(rows, query_tiles, key_tiles, value_tiles, out_tiles, grad_tiles, log_sum_exp):
@@ -350,8 +366,9 @@
         functools.partial(kernel, rows),
         out_shape=jax.ShapeDtypeStruct((3,) + flat, bf),
         in_specs=[pl.BlockSpec(memory_space=pltpu.HBM)] * 6,
-        out_specs=pl.BlockSpec(memory_space=pltpu.VMEM),
+        out_specs=pl.BlockSpec(memory_space=pltpu.HBM),
         scratch_shapes=[
+            pltpu.VMEM((3,) + flat, bf),
             pltpu.VMEM((6, tile, dim), bf),
             pltpu.VMEM((6, tile, dim), bf),
             pltpu.VMEM((6, 2, tile), f32),
@@ -381,6 +398,7 @@
             dma((3, 2)),
             dma((2, 3)),
             dma((2, 2, 2)),
+            dma((3, heads)),
         ],
         compiler_params=pltpu.CompilerParams(
             collective_id=0, has_side_effects=True, vmem_limit_bytes=60 * 2**20

time: 24.2 us -> 24.1 us (level)
  no operation moved by 1% of the time
where the time goes in v4:
time: 24.1 us; the launch traced here: 23.9 us
  Pallas kernels  21.3 us (88%)
  local copies, waits for them, and re-layouts  1.94 us (8%)
  between operations  0.64 us (3%)
    pallas_call x1, Pallas kernels, body(): pl.pallas_call(functools.partial(kernel, rows), out_shape=jax.ShapeDtypeS...  21.3 us
    unnamed x1, local copies, waits for them, and re-layouts  1.94 us

profile of v4, /device:TPU:1, one launch (start us, length us, event | category | flops | bytes accessed | tf_op | source)
XLA Modules:
  0.0 23.9 jit_solution(8415201705831007162)
XLA Ops:
  0.6 21.3 %tile_attention_backward.1 = bf16[3,2,384,128]{3,2,1,0:T(8,128)(2,1)} custom-call(bf16[2,384,128]{2,1,0:T(8,128)(2,1)} %bitcast.17, bf16[2,384,128]{2,1,0:T(8,128)(2,1)} %bitcast.18, bf16[2,384,128]{2,1,0:T(8,128)(2,1)} %bitcast.19, bf16[2,384,128]{2,1,0:T(8,128)(2,1)} %bitcast.20, bf16[2,384,128]{2,1,0:T(8,128)(2,1)} %bitcast.21, f32[2,1,1,1,384]{4,3,2,1,0:T(1,128)} %lse_ref.1), custom_call_target="tpu_custom_call" | custom-call | flops 2831155200 | bytes 1572864 | tf_op jit(solution)/shard_map/tile_attention_backward/pallas_call | solution.py:365
  22.0 1.9 %slice_bitcast_fusion = (bf16[2,1,1,1,384,128]{5,4,3,2,1,0:T(8,128)(2,1)}, bf16[2,1,1,1,384,128]{5,4,3,2,1,0:T(8,128)(2,1)}, bf16[2,1,1,1,384,128]{5,4,3,2,1,0:T(8,128)(2,1)}) fusion(bf16[3,2,384,128]{3,2,1,0:T(8,128)(2,1)} %tile_attention_backward.1), kind=kLoop, calls=%fused_computation | loop fusion | bytes 1179648
